TPU v7x, 32 devices: a whole 2x2x4 slice. The times are simulated.
32 devices in a mesh: trow: 8 (over y, x, core), tcol: 4 (over z).
Axes of the slice: x: 2, y: 2, z: 4, core: 2. Of those that a mesh axis runs over, the one named last changes fastest.
Arguments:
- left_factors: bfloat16 [2, 2, 16384, 1536], P(None, None, 'trow', 'tcol'), may hold values from -0.15625 to 0.15625
- right_factors: bfloat16 [2, 2, 6144, 4096], P(None, None, 'tcol', 'trow'), may hold values from -0.375 to 0.375
- ranks: int32 [2, 64, 24], P(None, 'trow', 'tcol'), may hold values from 4 to 64, as said below
- v_current: float32 [2, 2, 6144, 128], P(None, None, ('tcol', 'trow')), may hold values from -32 to 32
- u_prev: float32 [2, 2, 16384, 128], P(None, None, ('trow', 'tcol')), may hold values from -32 to 32
- alpha_prev: float32 [1], replicated, may hold values from 0.5 to 2
Outputs:
- u_next: float32 [2, 2, 16384, 128], P(None, None, ('trow', 'tcol'))
- v_next: float32 [2, 2, 6144, 128], P(None, None, ('tcol', 'trow'))
- scales: float32 [2], replicated
Inputs may be any that keep to these rules, and one draw needn't show every extreme that they name: `ranks`: for frequency f, tile (i, j) has rank 64 // 2 + 1 to 64 where |i * 24 - j * 64| < 192, and rank 4 to 32 elsewhere.
All inputs are finite; a program needn't handle non-finite values.
Results may differ from a plain program's by a relative error of at most 0.0028.
Values may be sent and summed in bfloat16 or wider, within the bound.
A program may use at most 128 MiB of HBM per device.

v0:
```python
import jax
import jax.numpy as jnp
from jax import lax
from jax.sharding import PartitionSpec as P

epsilon = 1e-06


def complex_product(form, a_real, a_imag, b_real, b_imag, conjugate):
    real_real = jnp.einsum(form, a_real, b_real, preferred_element_type=jnp.float32)
    imag_imag = jnp.einsum(form, a_imag, b_imag, preferred_element_type=jnp.float32)
    real_imag = jnp.einsum(form, a_real, b_imag, preferred_element_type=jnp.float32)
    imag_real = jnp.einsum(form, a_imag, b_real, preferred_element_type=jnp.float32)
    if conjugate:
        return (real_real + imag_imag, real_imag - imag_real)
    return (real_real - imag_imag, real_imag + imag_real)


def tile_views(left_factors, right_factors, rank_mask):
    frequencies = left_factors.shape[0]
    columns = rank_mask.shape[1]
    row_tiles = rank_mask.shape[2]
    tile_rows = right_factors.shape[2] // columns
    right_tiles = right_factors.reshape(frequencies, 2, columns, tile_rows, row_tiles, -1)
    left_tiles = left_factors.reshape(frequencies, 2, row_tiles, tile_rows, columns, -1)
    weight = rank_mask[..., None]
    return (left_tiles, right_tiles, weight, tile_rows)


def forward_tiles(gathered, left_factors, right_factors, rank_mask):
    left_tiles, right_tiles, weight, tile_rows = tile_views(left_factors, right_factors, rank_mask)
    frequencies = gathered.shape[0]
    sources = gathered.reshape(frequencies, 2, rank_mask.shape[1], tile_rows, -1)
    proj_real, proj_imag = complex_product(
        "fcmir,fcmn->fcirn",
        right_tiles[:, 0],
        right_tiles[:, 1],
        sources[:, 0],
        sources[:, 1],
        True,
    )
    proj_real = (proj_real * weight).astype(jnp.bfloat16)
    proj_imag = (proj_imag * weight).astype(jnp.bfloat16)
    out_real, out_imag = complex_product(
        "fimcr,fcirn->fimn", left_tiles[:, 0], left_tiles[:, 1], proj_real, proj_imag, False
    )
    return jnp.stack([out_real, out_imag], 1).reshape(
        frequencies, 2, rank_mask.shape[2] * tile_rows, -1
    )


def adjoint_tiles(targets, left_factors, right_factors, rank_mask):
    left_tiles, right_tiles, weight, tile_rows = tile_views(left_factors, right_factors, rank_mask)
    frequencies = targets.shape[0]
    blocks = targets.reshape(frequencies, 2, rank_mask.shape[2], tile_rows, -1)
    back_real, back_imag = complex_product(
        "fimcr,fimn->fcirn", left_tiles[:, 0], left_tiles[:, 1], blocks[:, 0], blocks[:, 1], True
    )
    back_real = (back_real * weight).astype(jnp.bfloat16)
    back_imag = (back_imag * weight).astype(jnp.bfloat16)
    out_real, out_imag = complex_product(
        "fcmir,fcirn->fcmn", right_tiles[:, 0], right_tiles[:, 1], back_real, back_imag, False
    )
    return jnp.stack([out_real, out_imag], 1).reshape(
        frequencies, 2, rank_mask.shape[1] * tile_rows, -1
    )


def body(left_factors, right_factors, ranks, v_current, u_prev, alpha_prev):
    rank_full = left_factors.shape[3] // ranks.shape[2]
    rank_mask = (
        jnp.arange(rank_full)[None, None, None, :] < jnp.transpose(ranks, (0, 2, 1))[..., None]
    ).astype(jnp.float32)
    devices = lax.axis_size("trow") * lax.axis_size("tcol")
    gathered = lax.all_gather(v_current.astype(jnp.bfloat16), "trow", axis=2, tiled=True)
    partial_value = forward_tiles(gathered, left_factors, right_factors, rank_mask)
    share_rows = u_prev.shape[2]
    col_start = lax.axis_index("tcol") * share_rows
    own_part = (
        lax.dynamic_slice_in_dim(partial_value, col_start, share_rows, 2) - alpha_prev[0] * u_prev
    )
    partial_value = lax.dynamic_update_slice_in_dim(partial_value, own_part, col_start, 2)
    count_u = u_prev.size * devices
    residual_u = lax.psum_scatter(partial_value, "tcol", scatter_dimension=2, tiled=True)
    squares = lax.psum(jnp.sum(residual_u * residual_u), ("trow", "tcol"))
    beta_scale = jnp.sqrt(squares / count_u + epsilon)
    u_next = residual_u / beta_scale
    targets = lax.all_gather(u_next.astype(jnp.bfloat16), "tcol", axis=2, tiled=True)
    partial_back = adjoint_tiles(targets, left_factors, right_factors, rank_mask)
    source_share = v_current.shape[2]
    row_start = lax.axis_index("trow") * source_share
    own_back = (
        lax.dynamic_slice_in_dim(partial_back, row_start, source_share, 2) - beta_scale * v_current
    )
    partial_back = lax.dynamic_update_slice_in_dim(partial_back, own_back, row_start, 2)
    residual_v = lax.psum_scatter(partial_back, "trow", scatter_dimension=2, tiled=True)
    squares_v = lax.psum(jnp.sum(residual_v * residual_v), ("trow", "tcol"))
    alpha_next = jnp.sqrt(squares_v / (v_current.size * devices) + epsilon)
    v_next = residual_v / alpha_next
    return (u_next, v_next, jnp.stack([beta_scale, alpha_next]))


def solution(mesh):
    return jax.shard_map(
        body,
        mesh=mesh,
        in_specs=(
            P(None, None, "trow", "tcol"),
            P(None, None, "tcol", "trow"),
            P(None, "trow", "tcol"),
            P(None, None, ("tcol", "trow"), None),
            P(None, None, ("trow", "tcol"), None),
            P(),
        ),
        out_specs=(
            P(None, None, ("trow", "tcol"), None),
            P(None, None, ("tcol", "trow"), None),
            P(),
        ),
        check_vma=False,
    )
```

profile of v0, /device:TPU:0, one launch (start us, length us, event | category | flops | bytes accessed | tf_op | source)
XLA Modules:
  0.0 400.4 jit_solution(12258209969093380117)
XLA Ops:
  7.2 1.7 convert_element_type.25
  9.0 16.3 %reshape.58 = bf16[2,2,6,256,8,64]{5,4,3,2,1,0:T(8,128)(2,1)} reshape(bf16[2,2,1536,512]{3,2,1,0:T(8,128)(2,1)} %param.7) | data formatting | bytes 12582912 | tf_op jit(solution)/shard_map/reshape | solution.py:24
  25.2 11.1 %fusion.62 = (bf16[2,1,6,256,8,64]{5,4,3,2,1,0:T(8,128)(2,1)}, bf16[2,1,6,256,8,64]{5,4,3,2,1,0:T(8,128)(2,1)}) fusion(bf16[2,2,6,256,8,64]{5,4,3,2,1,0:T(8,128)(2,1)} %reshape.58), kind=kLoop, calls=%fused_computation.78 | loop fusion | bytes 12582912 | tf_op jit(solution)/shard_map/slice | solution.py:36
  36.4 5.8 %copy.57 = bf16[2,1,6,256,8,64]{3,5,4,2,0,1:T(8,128)(2,1)S(1)} copy(bf16[2,1,6,256,8,64]{5,4,3,2,1,0:T(8,128)(2,1)} %get-tuple-element.9) | data formatting | bytes 6291456
  42.2 7.1 %copy.56 = bf16[2,1,6,256,8,64]{3,5,4,2,0,1:T(8,128)(2,1)} copy(bf16[2,1,6,256,8,64]{5,4,3,2,1,0:T(8,128)(2,1)} %get-tuple-element.8) | data formatting | bytes 6291456
  49.3 8.7 %copy.25 = bf16[2,2,2048,384]{2,3,1,0:T(8,128)(2,1)} copy(bf16[2,2,2048,384]{3,2,1,0:T(8,128)(2,1)} %param.6) | data formatting | bytes 12582912 | tf_op args[0]
  58.0 8.2 %copy.60 = bf16[192,8,8,256]{3,2,1,0:T(8,128)(2,1)} copy(bf16[192,8,8,256]{3,1,2,0:T(8,128)(2,1)} %bitcast.153) | data formatting | bytes 12582912
  67.0 6.1 %fusion.63 = (bf16[2,1,8,256,6,64]{3,2,5,4,1,0:T(8,128)(2,1)}, bf16[2,1,8,256,6,64]{3,2,5,4,1,0:T(8,128)(2,1)}) fusion(bf16[2,2,8,256,6,64]{3,2,5,4,1,0:T(8,128)(2,1)} %bitcast.152), kind=kLoop, calls=%fused_computation.79 | loop fusion | bytes 12582912 | tf_op jit(solution)/shard_map/slice | solution.py:45
  73.1 1.5 copy.22
  74.6 1.0 fusion.14
  75.6 1.0 fusion.16
  76.6 0.9 copy-done
  77.5 1.2 multiply_convert_fusion
  78.7 1.4 multiply_convert_fusion.1
  80.1 1.0 copy-done.4
  81.1 1.2 fusion.4
  82.3 2.5 fusion.2
  84.8 2.6 fusion.27
  87.5 2.9 copy.30
  90.4 5.6 %fusion.26 = f32[2,8,256,128]{2,3,1,0:T(8,128)} fusion(f32[2,8,128,256,1]{3,2,4,1,0:T(8,128)} %fusion.2, bf16[2,6,8,64,128]{4,3,2,1,0:T(8,128)(2,1)} %copy-done.12, bf16[2,1,8,256,6,64]{3,2,5,4,1,0:T(8,128)(2,1)} %get-tuple-element.10), kind=kOutput, calls=%fused_computation.39 | convolution fusion | flops 403177472 | bytes 8912896 | tf_op jit(solution)/shard_map/fimcr,fcirn->fimn/dot_general | solution.py:12
  96.0 2.9 copy.33
  98.9 4.6 %pad_maximum_fusion = f32[2,2,2048,128]{3,2,0,1:T(8,128)} fusion(f32[2,1,2048,128]{3,2,0,1:T(8,128)} %bitcast.156, f32[2,1,2048,128]{3,2,0,1:T(8,128)} %bitcast.154), kind=kLoop, calls=%fused_computation.1 | loop fusion | flops 1048576 | bytes 8388608 | tf_op jit(solution)/shard_map/stack | solution.py:47
  103.5 1.1 fusion.48
  104.7 79.5 %reduce-scatter.3.cloned.1.call-done = f32[2,2,512,128]{3,2,0,1:T(8,128)} async-done(((f32[2,2,2048,128]{3,2,0,1:T(8,128)}), f32[2,2,512,128]{3,2,0,1:T(8,128)}) %reduce-scatter.3.cloned.1.call-update) | async-done | bytes 1048592 | tf_op jit(solution)/shard_map/reduce_scatter | solution.py:84
  184.3 2.1 multiply_reduce_fusion
  186.4 40.9 %psum.14 = f32[]{:T(128)} all-reduce(f32[]{:T(128)} %multiply_reduce_fusion), channel_id=1, replica_groups=mesh['trow'=8,'tcol'=4] {'trow','tcol'}, use_global_device_ids=true, to_apply=%region_2.0 | all-reduce | flops 1 | bytes 8 | tf_op jit(solution)/shard_map/psum | solution.py:85
  228.0 2.5 fusion.61
  230.6 4.5 %copy.58 = bf16[2,1,8,256,6,64]{3,5,4,2,0,1:T(8,128)(2,1)} copy(bf16[2,1,8,256,6,64]{3,2,5,4,1,0:T(8,128)(2,1)} %get-tuple-element.10) | data formatting | bytes 6291456
  235.1 2.5 copy.59
  237.5 39.1 %all-gather.5.cloned.1.call-done = bf16[2,2,2048,128]{3,2,0,1:T(8,128)(2,1)} async-done(((bf16[2,2,512,128]{3,2,0,1:T(8,128)(2,1)}), bf16[2,2,2048,128]{3,2,0,1:T(8,128)(2,1)}) %all-gather.5.cloned.1.call-update) | async-done | bytes 2097168 | tf_op jit(solution)/shard_map/all_gather | solution.py:88
  276.6 3.3 fusion.49
  280.4 1.0 fusion.52
  281.4 0.9 copy-done.6
  282.3 1.0 fusion.51
  283.3 1.0 fusion.50
  284.3 1.9 fusion
  287.4 1.9 fusion.10
  289.8 1.9 fusion.37
  291.8 3.2 copy.39
  294.9 3.7 fusion.36
  298.7 2.0 copy.40
  300.7 1.9 pad_maximum_fusion.1
  302.6 0.8 fusion.55
  303.4 45.1 %reduce-scatter.5.cloned.1.call-done = f32[2,2,192,128]{3,2,0,1:T(8,128)} async-done(((f32[2,2,1536,128]{3,2,0,1:T(8,128)}), f32[2,2,192,128]{3,2,0,1:T(8,128)}) %reduce-scatter.5.cloned.1.call-update) | async-done | bytes 393232 | tf_op jit(solution)/shard_map/reduce_scatter | solution.py:96
  348.5 1.7 multiply_reduce_fusion.1
  350.2 1.0 copy.42
  351.3 39.5 %psum.15 = f32[]{:T(128)} all-reduce(f32[]{:T(128)} %multiply_reduce_fusion.1), channel_id=1, replica_groups=mesh['trow'=8,'tcol'=4] {'trow','tcol'}, use_global_device_ids=true, to_apply=%region_5.0 | all-reduce | flops 1 | bytes 8 | tf_op jit(solution)/shard_map/psum | solution.py:97
  391.5 1.0 broadcast_divide_fusion.1
  (47 shorter events, 4.0 us)
Async XLA Ops:
  7.2 65.9 %all-gather.3.cloned.1.call-start = ((), (), s32[]{:S(2)}) async-start(), calls=%async_computation.2 | async-start | bytes 1769472 | tf_op jit(solution)/shard_map/all_gather | solution.py:75
  8.9 175.3 %reduce-scatter.3.cloned.1.call-start = ((), (), s32[]{:S(2)}) async-start(), calls=%async_computation.3 | async-start | bytes 5242880 | tf_op jit(solution)/shard_map/reduce_scatter | solution.py:84
  42.2 7.1 %copy-start.17 = (s32[2,8,6]{1,0,2:T(2,128)S(1)}, s32[2,8,6]{1,0,2:T(2,128)}, u32[]{:S(2)}) copy-start(s32[2,8,6]{1,0,2:T(2,128)} %param.8) | copy-start | bytes 1156
  75.6 1.9 copy-start
  78.7 1.4 copy-start.12
  78.7 2.5 copy-start.4
  82.3 2.5 copy-start.3
  98.9 4.6 %copy-start.8 = (f32[2,8,256,128]{3,2,1,0:T(8,128)S(1)}, f32[2,8,256,128]{3,2,1,0:T(8,128)}, u32[]{:S(2)}) copy-start(f32[2,8,256,128]{3,2,1,0:T(8,128)} %copy.30) | copy-start | bytes 6291460
  98.9 4.6 %copy-start.9 = (f32[2,8,256,128]{3,2,1,0:T(8,128)S(1)}, f32[2,8,256,128]{3,2,1,0:T(8,128)}, u32[]{:S(2)}) copy-start(f32[2,8,256,128]{3,2,1,0:T(8,128)} %copy.33) | copy-start | bytes 6291460
  98.9 4.6 %copy-start.16 = (f32[2,2,512,128]{3,2,1,0:T(8,128)S(1)}, f32[2,2,512,128]{3,2,1,0:T(8,128)}, u32[]{:S(2)}) copy-start(f32[2,2,512,128]{3,2,1,0:T(8,128)} %param.10) | copy-start | bytes 3145732
  104.7 171.9 %all-gather.5.cloned.1.call-start = ((), (), s32[]{:S(2)}) async-start(), calls=%async_computation.4 | async-start | bytes 2621440 | tf_op jit(solution)/shard_map/all_gather | solution.py:88
  230.5 118.0 %reduce-scatter.5.cloned.1.call-start = ((), (), s32[]{:S(2)}) async-start(), calls=%async_computation.5 | async-start | bytes 3538944 | tf_op jit(solution)/shard_map/reduce_scatter | solution.py:96
  230.6 4.5 %copy-start.5 = (bf16[2,1,8,256,6,64]{3,2,5,4,1,0:T(8,128)(2,1)S(1)}, bf16[2,1,8,256,6,64]{3,2,5,4,1,0:T(8,128)(2,1)}, u32[]{:S(2)}) copy-start(bf16[2,1,8,256,6,64]{3,2,5,4,1,0:T(8,128)(2,1)} %get-tuple-element.11) | copy-start | bytes 9437188
  276.6 3.3 copy-start.7
  276.6 3.8 copy-start.13
  280.4 1.9 copy-start.6
  286.2 1.2 copy-start.11
  287.4 2.5 copy-start.1
  291.8 3.2 copy-start.2
  298.7 2.0 copy-start.10
  300.7 1.9 copy-start.15
  303.4 46.8 %copy-start.14 = (f32[2,2,512,128]{3,2,0,1:T(8,128)S(1)}, f32[2,2,512,128]{3,2,0,1:T(8,128)}, u32[]{:S(2)}) copy-start(f32[2,2,512,128]{3,2,0,1:T(8,128)} %get-tuple-element.7) | copy-start | bytes 3145732
Sparse Core Ops, SparseCore 0:
  10.5 28.3 all-gather.2
  104.8 79.4 reduce-scatter.2
  230.7 45.8 all-gather.4
  303.5 44.9 reduce-scatter.4
where the time goes:
time: 402 us; the launch traced here: 400 us
  waiting for transfers between devices  164 us (41%)
  local copies, waits for them, and re-layouts  88.9 us (22%)
  blocking collectives  80.5 us (20%)
  matrix products  31 us (8%)
  other arithmetic  20 us (5%)
  between operations  16 us (4%)
    reduce_scatter x1, waiting for transfers between devices, body(): lax.psum_scatter(partial_value, 'tcol', scatter_dimension=2, tiled=True)  79.5 us
    reduce_scatter x1, waiting for transfers between devices, body(): lax.psum_scatter(partial_back, 'trow', scatter_dimension=2, tiled=True)  45.1 us
    unnamed x44, local copies, waits for them, and re-layouts  43 us
    psum x1, blocking collectives, body(): squares = lax.psum(jnp.sum(residual_u * residual_u), ('trow', 'tcol'))  40.9 us
    psum x1, blocking collectives, body(): squares_v = lax.psum(jnp.sum(residual_v * residual_v), ('trow', 'tcol'))  39.5 us
    all_gather x1, waiting for transfers between devices, body(): lax.all_gather(u_next.astype(jnp.bfloat16), 'tcol', axis=2, tiled=True)  39.1 us
    reshape x1, local copies, waits for them, and re-layouts, tile_views(): right_factors.reshape(frequencies, 2, columns, tile_rows, row_tiles, -1)  16.3 us
    slice x1, local copies, waits for them, and re-layouts, forward_tiles(): right_tiles[:, 0]  11.1 us
  transfers between devices with their start and end apart: 4, of which 3 were waited for; matrix products, arithmetic and copies ran while one was open for 18% of the time, Pallas kernels for 0%

commit v1 on v0

v1 whole, which is shorter than its diff:
```python
import functools
import math

import jax
import jax.numpy as jnp
from jax import lax
from jax.experimental import pallas as pl
from jax.experimental.pallas import tpu as pltpu
from jax.sharding import PartitionSpec as P

epsilon = 1e-06
MESH = pl.DeviceIdType.MESH
BF16 = jnp.bfloat16
F32 = jnp.float32


def kernel(
    R, C,
    left_hbm, right_hbm, ranks, v_cur, u_prev_hbm, alpha_prev,
    u_next, v_next, scales,
    left, right, u_prev, sslot, sfull, proj, part, back, vfull,
    rbuf, lbuf, tbuf, vsend, vrecv, norm_r, norm_c,
    load_sem, gs_sem, gr_sem, rs_sem, rr_sem, ls_sem, lr_sem,
    tr_sem, tl_sem, tt_sem, vs_sem, vr_sem, nrs_sem, nrr_sem, ncs_sem, ncr_sem,
):
    F, _, MTl, NTl = (left.shape[0], 2, ranks.shape[1], ranks.shape[2])
    rows_u, rows_v = left.shape[2], right.shape[2]
    T = rows_u // MTl
    K = left.shape[3] // NTl
    KR, KL = MTl * K, NTl * K
    ur, sr, nv = u_prev.shape[2], v_cur.shape[2], v_cur.shape[3]
    tiles = ur // T
    n = int(math.log2(R))
    r = lax.axis_index("trow")
    c = lax.axis_index("tcol")

    orders = ([0] + list(range(n - 1, 0, -1)), [0] + list(range(1, n)))

    def flip(bit):
        return (1 - 2 * ((r // 2**bit) % 2)) * 2**bit

    def owner(p, q):
        b = r
        for k in range(n):
            if (q >> (n - 1 - k)) & 1:
                b = b + flip(orders[p][k])
        return b

    def rows_of(p, q):
        return pl.ds(pl.multiple_of(owner(p, q) * sr, sr), sr)

    def tile_rows(i):
        return pl.ds(pl.multiple_of(i * T, T), T)

    def to(row, col):
        return (row, col)

    def remote(src, dst, ssem, rsem, dev):
        return pltpu.make_async_remote_copy(
            src_ref=src, dst_ref=dst, send_sem=ssem, recv_sem=rsem, device_id=dev, device_id_type=MESH
        )

    barrier = pltpu.get_barrier_semaphore()
    for d in range(1, R):
        pl.semaphore_signal(barrier, inc=1, device_id=to(lax.rem(r + d, R), c), device_id_type=MESH)
    for d in range(1, C):
        pl.semaphore_signal(barrier, inc=1, device_id=to(r, lax.rem(c + d, C)), device_id_type=MESH)

    loads = []
    for f in range(F):
        loads.append(
            (
                pltpu.make_async_copy(right_hbm.at[f], right.at[f], load_sem.at[2 * f]),
                pltpu.make_async_copy(left_hbm.at[f], left.at[f], load_sem.at[2 * f + 1]),
            )
        )
    load_u = pltpu.make_async_copy(u_prev_hbm, u_prev, load_sem.at[2 * F])
    for f in range(F):
        loads[f][0].start()
        loads[f][1].start()
    load_u.start()
    for f in range(F):
        for p in range(2):
            sslot[f, p, 0] = v_cur[f, p].astype(BF16)
    pl.semaphore_wait(barrier, R + C - 2)

    def gather_copy(f, p, m):
        bit = orders[p][n - 1 - m]
        size = 2**m
        return remote(
            sslot.at[f, p, pl.ds(0, size)], sslot.at[f, p, pl.ds(size, size)],
            gs_sem.at[f, p, m], gr_sem.at[f, p, m], to(r + flip(bit), c),
        )

    def gather_start(f, m):
        for p in range(2):
            gather_copy(f, p, m).start()

    def gather_wait(f, m):
        for p in range(2):
            gather_copy(f, p, m).wait()

    def project(f):
        for p in range(2):
            for q in range(R):
                sfull[p, rows_of(p, q), :] = sslot[f, p, q]

        def step(j, carry):
            rows = tile_rows(j)
            s_real, s_imag = sfull[0, rows, :], sfull[1, rows, :]
            weights = jnp.concatenate(
                [
                    jnp.concatenate([s_real, s_imag], 1),
                    jnp.concatenate([s_imag, -s_real], 1),
                ],
                0,
            )
            factors = jnp.concatenate([right[f, 0, rows, :], right[f, 1, rows, :]], 0)
            value = lax.dot_general(factors, weights, (((0,), (0,)), ((), ())), preferred_element_type=F32)
            index = lax.broadcasted_iota(jnp.int32, (K, 2 * nv), 0)
            for i in range(MTl):
                kept = jnp.where(index < ranks[f, i, j], value[i * K : (i + 1) * K], 0.0)
                turned = jnp.concatenate([-kept[:, nv:], kept[:, :nv]], 1)
                proj[i, pl.ds(pl.multiple_of(j * K, K), K), :] = kept.astype(BF16)
                proj[i, pl.ds(pl.multiple_of(KL + j * K, K), K), :] = turned.astype(BF16)
            return carry

        lax.fori_loop(0, NTl, step, 0)

    def image_block(f, b):
        def step(t, carry):
            i = b * tiles + t
            rows = tile_rows(i)
            factors = jnp.concatenate([left[f, 0, rows, :], left[f, 1, rows, :]], 1)
            part[f, rows, :] = jnp.dot(factors, proj[i], preferred_element_type=F32)
            return carry

        lax.fori_loop(0, tiles, step, 0)

    def block_rows(b):
        return pl.ds(pl.multiple_of(b * ur, ur), ur)

    def right_copy(f, b):
        return remote(rbuf.at[f, b], rbuf.at[f, b], rs_sem.at[f, b], rr_sem.at[f, b], to(r, lax.rem(c + 1, C)))

    def left_copy(f, b):
        return remote(lbuf.at[f, b], lbuf.at[f, b], ls_sem.at[f, b], lr_sem.at[f, b], to(r, lax.rem(c + C - 1, C)))

    def images(f):
        def step(s, carry):
            b = jnp.where(c < C // 2, C - 1 - s, s)
            image_block(f, b)

            @pl.when((c == 0) & (b > 0))
            def _():
                for p in range(2):
                    rbuf[f, b, p] = part[f, block_rows(b), p * nv : (p + 1) * nv].astype(BF16)
                right_copy(f, b).start()

            @pl.when((c == C - 1) & (b < C - 1))
            def _():
                for p in range(2):
                    lbuf[f, b, p] = part[f, block_rows(b), p * nv : (p + 1) * nv].astype(BF16)
                left_copy(f, b).start()

            return carry

        lax.fori_loop(0, C, step, 0)

    def pass_sums(f, s):
        b = C - 1 - s

        @pl.when((c > 0) & (c < b))
        def _():
            right_copy(f, b).wait_recv()
            for p in range(2):
                rbuf[f, b, p] = (
                    rbuf[f, b, p].astype(F32) + part[f, block_rows(b), p * nv : (p + 1) * nv]
                ).astype(BF16)
            right_copy(f, b).start()

        @pl.when((c > s) & (c < C - 1))
        def _():
            left_copy(f, s).wait_recv()
            for p in range(2):
                lbuf[f, s, p] = (
                    lbuf[f, s, p].astype(F32) + part[f, block_rows(s), p * nv : (p + 1) * nv]
                ).astype(BF16)
            left_copy(f, s).start()

    def give_right(f, b):
        return remote(tbuf.at[f, b], tbuf.at[f, b], tr_sem.at[f, b], tt_sem.at[f, b], to(r, lax.rem(c + 1, C)))

    def give_left(f, b):
        return remote(tbuf.at[f, b], tbuf.at[f, b], tl_sem.at[f, b], tt_sem.at[f, b], to(r, lax.rem(c + C - 1, C)))

    def squares(value):
        return jnp.sum((value * value).reshape(-1, 8, nv), axis=0)

    def finish_sums(f, total):
        @pl.when(c > 0)
        def _():
            right_copy(f, c).wait_recv()
            for p in range(2):
                lanes = slice(p * nv, (p + 1) * nv)
                part[f, block_rows(c), lanes] = part[f, block_rows(c), lanes] + rbuf[f, c, p].astype(F32)

        @pl.when(c < C - 1)
        def _():
            left_copy(f, c).wait_recv()
            for p in range(2):
                lanes = slice(p * nv, (p + 1) * nv)
                part[f, block_rows(c), lanes] = part[f, block_rows(c), lanes] + lbuf[f, c, p].astype(F32)

        for p in range(2):
            value = part[f, block_rows(c), p * nv : (p + 1) * nv] - alpha_prev[0] * u_prev[f, p]
            u_next[f, p] = value
            tbuf[f, c, p] = value.astype(BF16)
            total = total + squares(value)

        @pl.when(c < C - 1)
        def _():
            give_right(f, c).start()

        @pl.when(c > 0)
        def _():
            give_left(f, c).start()

        return total

    def pass_targets(f, s, then):
        @pl.when(c >= s)
        def _():
            b = c - s
            give_right(f, b).wait_recv()

            @pl.when(c < C - 1)
            def _():
                give_right(f, b).start()

            then(b)

        @pl.when(c + s < C)
        def _():
            b = c + s
            give_left(f, b).wait_recv()

            @pl.when(c > 0)
            def _():
                give_left(f, b).start()

            then(b)

    def norm_row(e, d):
        other = lax.rem(r + d, R)
        return remote(norm_r.at[e, r], norm_r.at[e, r], nrs_sem.at[e, d], nrr_sem.at[e, r], to(other, c))

    def norm_row_in(e, d):
        other = lax.rem(r + d, R)
        return remote(norm_r.at[e, other], norm_r.at[e, other], nrs_sem.at[e, d], nrr_sem.at[e, other], to(other, c))

    def norm_col(e, d):
        other = lax.rem(c + d, C)
        return remote(norm_c.at[e, c], norm_c.at[e, c], ncs_sem.at[e, d], ncr_sem.at[e, c], to(r, other))

    def norm_col_in(e, d):
        other = lax.rem(c + d, C)
        return remote(norm_c.at[e, other], norm_c.at[e, other], ncs_sem.at[e, d], ncr_sem.at[e, other], to(r, other))

    def norm_start(e, total):
        norm_r[e, r] = total
        for d in range(1, R):
            norm_row(e, d).start()

    def norm_finish(e, count):
        for d in range(1, R):
            norm_row_in(e, d).wait_recv()
        row_total = norm_r[e, 0]
        for d in range(1, R):
            row_total = row_total + norm_r[e, d]
        norm_c[e, c] = row_total
        for d in range(1, C):
            norm_col(e, d).start()
        for d in range(1, C):
            norm_col_in(e, d).wait_recv()
        total = norm_c[e, 0]
        for d in range(1, C):
            total = total + norm_c[e, d]
        return jnp.sqrt(jnp.sum(total, keepdims=True) / count + epsilon)

    def back_block(f, inverse):
        def run(b):
            def step(t, carry):
                i = b * tiles + t
                rows = tile_rows(i)
                inner = tile_rows(t)
                t_real, t_imag = tbuf[f, b, 0, inner, :], tbuf[f, b, 1, inner, :]
                weights = jnp.concatenate(
                    [
                        jnp.concatenate([t_real, t_imag], 1),
                        jnp.concatenate([t_imag, -t_real], 1),
                    ],
                    0,
                )
                factors = jnp.concatenate([left[f, 0, rows, :], left[f, 1, rows, :]], 0)
                value = lax.dot_general(factors, weights, (((0,), (0,)), ((), ())), preferred_element_type=F32)
                value = value * inverse
                index = lax.broadcasted_iota(jnp.int32, (K, 2 * nv), 0)
                for j in range(NTl):
                    kept = jnp.where(index < ranks[f, i, j], value[j * K : (j + 1) * K], 0.0)
                    turned = jnp.concatenate([-kept[:, nv:], kept[:, :nv]], 1)
                    back[j, pl.ds(pl.multiple_of(i * K, K), K), :] = kept.astype(BF16)
                    back[j, pl.ds(pl.multiple_of(KR + i * K, K), K), :] = turned.astype(BF16)
                return carry

            lax.fori_loop(0, tiles, step, 0)

        return run

    def back_image(f):
        def step(j, carry):
            rows = tile_rows(j)
            factors = jnp.concatenate([right[f, 0, rows, :], right[f, 1, rows, :]], 1)
            vfull[f, rows, :] = jnp.dot(factors, back[j], preferred_element_type=F32)
            return carry

        lax.fori_loop(0, NTl, step, 0)

    def halve_copy(f, p, k):
        half = R >> (k + 1)
        return remote(
            vsend.at[f, p, pl.ds(half, half)], vrecv.at[f, p, pl.ds(half, half)],
            vs_sem.at[f, p, k], vr_sem.at[f, p, k], to(r + flip(orders[p][k]), c),
        )

    def halve_start(f, k):
        half = R >> (k + 1)
        for p in range(2):
            for q in range(half, 2 * half):
                vsend[f, p, q] = vfull[f, rows_of(p, q), p * nv : (p + 1) * nv]
            halve_copy(f, p, k).start()

    def halve_wait(f, k):
        half = R >> (k + 1)
        for p in range(2):
            halve_copy(f, p, k).wait_recv()
            lanes = slice(p * nv, (p + 1) * nv)
            for q in range(half):
                rows = rows_of(p, q)
                vfull[f, rows, lanes] = vfull[f, rows, lanes] + vrecv[f, p, half + q]

    def halve_next(f, k):
        halve_wait(f, k)
        if k + 1 < n:
            halve_start(f, k + 1)

    for m in range(n):
        gather_start(0, m)
        gather_wait(0, m)
    for f in range(F):
        if f + 1 < F:
            gather_start(f + 1, 0)
        loads[f][0].wait()
        project(f)
        if f + 1 < F:
            gather_wait(f + 1, 0)
            gather_start(f + 1, 1)
        loads[f][1].wait()
        images(f)
        if f + 1 < F:
            for m in range(1, n):
                if m > 1:
                    gather_start(f + 1, m)
                gather_wait(f + 1, m)
    load_u.wait()
    nothing = lambda b: None
    total = jnp.zeros((8, nv), F32)
    for f in range(F):
        for s in range(C - 1):
            pass_sums(f, s)
            if f > 0:
                pass_targets(f - 1, s + 1, nothing)
        total = finish_sums(f, total)
    norm_start(0, total)
    count_u = F * 2 * ur * nv * R * C
    beta = norm_finish(0, count_u)
    inverse = 1.0 / beta

    for f in range(F):
        run = back_block(f, inverse)
        if f < F - 1:
            lax.fori_loop(0, C, lambda b, carry: (run(b), carry)[1], 0)
        else:
            run(c)
            for s in range(1, C):
                pass_targets(f, s, run)
                if f > 0 and s < n:
                    halve_next(f - 1, s - 1)
            if f > 0:
                for k in range(min(C - 1, n - 1), n):
                    halve_next(f - 1, k)
        back_image(f)
        halve_start(f, 0)
    for k in range(n):
        halve_next(F - 1, k)
    total = jnp.zeros((8, nv), F32)
    for f in range(F):
        for p in range(2):
            value = vfull[f, rows_of(p, 0), p * nv : (p + 1) * nv] - beta * v_cur[f, p]
            v_next[f, p] = value
            total = total + squares(value)
    norm_start(1, total)
    for f in range(F):
        for p in range(2):
            u_next[f, p] = u_next[f, p] / beta
    alpha = norm_finish(1, F * 2 * sr * nv * R * C)
    for f in range(F):
        for p in range(2):
            v_next[f, p] = v_next[f, p] / alpha
    scales[0] = beta[0, 0]
    scales[1] = alpha[0, 0]

    for f in range(F):
        for s in range(C):

            @pl.when(c < s)
            def _():
                right_copy(f, s).wait_send()

            @pl.when(c > s)
            def _():
                left_copy(f, s).wait_send()

            @pl.when((s <= c) & (c < C - 1))
            def _():
                give_right(f, s).wait_send()

            @pl.when((s >= c) & (c > 0))
            def _():
                give_left(f, s).wait_send()

        for p in range(2):
            for k in range(n):
                halve_copy(f, p, k).wait_send()
    for e in range(2):
        for d in range(1, R):
            norm_row(e, d).wait_send()
        for d in range(1, C):
            norm_col(e, d).wait_send()


def body(R, C, left_factors, right_factors, ranks, v_current, u_prev, alpha_prev):
    F, _, rows_u, KL = left_factors.shape
    rows_v, KR = right_factors.shape[2:]
    MTl, NTl = ranks.shape[1:]
    sr, nv = v_current.shape[2:]
    ur = u_prev.shape[2]
    n = int(math.log2(R))
    dma = pltpu.SemaphoreType.DMA
    anywhere = pl.BlockSpec(memory_space=pl.ANY)
    vmem = pl.BlockSpec(memory_space=pltpu.VMEM)
    smem = pl.BlockSpec(memory_space=pltpu.SMEM)
    flops = 8 * 2 * F * nv * rows_u * KL * 2
    return pl.pallas_call(
        functools.partial(kernel, R, C),
        out_shape=(
            jax.ShapeDtypeStruct(u_prev.shape, F32),
            jax.ShapeDtypeStruct(v_current.shape, F32),
            jax.ShapeDtypeStruct((2,), F32),
        ),
        in_specs=[anywhere, anywhere, smem, vmem, anywhere, smem],
        out_specs=(vmem, vmem, smem),
        scratch_shapes=[
            pltpu.VMEM(left_factors.shape, BF16),
            pltpu.VMEM(right_factors.shape, BF16),
            pltpu.VMEM(u_prev.shape, F32),
            pltpu.VMEM((F, 2, R, sr, nv), BF16),
            pltpu.VMEM((2, rows_v, nv), BF16),
            pltpu.VMEM((MTl, 2 * KL, 2 * nv), BF16),
            pltpu.VMEM((F, rows_u, 2 * nv), F32),
            pltpu.VMEM((NTl, 2 * KR, 2 * nv), BF16),
            pltpu.VMEM((F, rows_v, 2 * nv), F32),
            pltpu.VMEM((F, C, 2, ur, nv), BF16),
            pltpu.VMEM((F, C, 2, ur, nv), BF16),
            pltpu.VMEM((F, C, 2, ur, nv), BF16),
            pltpu.VMEM((F, 2, R, sr, nv), F32),
            pltpu.VMEM((F, 2, R, sr, nv), F32),
            pltpu.VMEM((2, R, 8, nv), F32),
            pltpu.VMEM((2, C, 8, nv), F32),
            dma((2 * F + 1,)),
            dma((F, 2, n)),
            dma((F, 2, n)),
            dma((F, C)),
            dma((F, C)),
            dma((F, C)),
            dma((F, C)),
            dma((F, C)),
            dma((F, C)),
            dma((F, C)),
            dma((F, 2, n)),
            dma((F, 2, n)),
            dma((2, R)),
            dma((2, R)),
            dma((2, C)),
            dma((2, C)),
        ],
        compiler_params=pltpu.CompilerParams(
            collective_id=0, has_side_effects=True, vmem_limit_bytes=56 * 1024 * 1024
        ),
        cost_estimate=pl.CostEstimate(flops=flops, bytes_accessed=16 * 1024 * 1024, transcendentals=0),
    )(left_factors, right_factors, ranks, v_current, u_prev, alpha_prev)


def solution(mesh):
    return jax.shard_map(
        functools.partial(body, mesh.shape["trow"], mesh.shape["tcol"]),
        mesh=mesh,
        in_specs=(
            P(None, None, "trow", "tcol"),
            P(None, None, "tcol", "trow"),
            P(None, "trow", "tcol"),
            P(None, None, ("tcol", "trow"), None),
            P(None, None, ("trow", "tcol"), None),
            P(),
        ),
        out_specs=(
            P(None, None, ("trow", "tcol"), None),
            P(None, None, ("tcol", "trow"), None),
            P(),
        ),
        check_vma=False,
    )
```

time: 402 us -> 141 us (0.35)
  waiting for transfers between devices: 164 us -> 0 us
  Pallas kernels: 0 us -> 133 us
  local copies, waits for them, and re-layouts: 88.9 us -> 6.58 us
  blocking collectives: 80.5 us -> 0 us
  matrix products: 31 us -> 0 us
  other arithmetic: 20 us -> 0 us
  between operations: 16 us -> 1.29 us
    pallas_call x0 -> x1, Pallas kernels: none -> 133 us  [body(): pl.pallas_call(functools.partial(kernel, R, C), out_shape=(jax.ShapeDtype...]
    reduce_scatter x2 -> x0, waiting for transfers between devices: 125 us -> none  [the longest x1 79.5 us: body(): lax.psum_scatter(partial_value, 'tcol', scatter_dimension=2, tiled=True)]
    psum x2 -> x0, blocking collectives: 80.5 us -> none  [the longest x1 40.9 us: body(): squares = lax.psum(jnp.sum(residual_u * residual_u), ('trow', 'tcol'))]
    all_gather x2 -> x0, waiting for transfers between devices: 39.1 us -> none  [the longest x1 39.1 us: body(): lax.all_gather(u_next.astype(jnp.bfloat16), 'tcol', axis=2, tiled=True)]
    unnamed x44 -> x4, local copies, waits for them, and re-layouts: 43 us -> 6.58 us
    dot_general x12 -> x0, matrix products: 24.8 us -> none  [the longest x3 10.6 us: complex_product(): jnp.einsum(form, a_real, b_imag, preferred_element_type=jnp.float32)]
    slice x2 -> x0, local copies, waits for them, and re-layouts: 17.2 us -> none  [the longest x1 11.1 us: forward_tiles(): right_tiles[:, 0]]
    reshape x1 -> x0, local copies, waits for them, and re-layouts: 16.3 us -> none  [tile_views(): right_factors.reshape(frequencies, 2, columns, tile_rows, row_tiles, -1)]
  transfers between devices with their start and end apart: 4 -> 0, of which waited for: 3 -> 0; matrix products, arithmetic and copies ran while one was open for 18% -> 0% of each run, Pallas kernels for 0% -> 0%
where the time goes in v1:
time: 141 us
  Pallas kernels  133 us (94%)
  local copies, waits for them, and re-layouts  6.58 us (5%)
    pallas_call x1, Pallas kernels, body(): pl.pallas_call(functools.partial(kernel, R, C), out_shape=(jax.ShapeDtype...  133 us
    unnamed x4, local copies, waits for them, and re-layouts  6.58 us

profile of v1, /device:TPU:0, one launch (start us, length us, event | category | flops | bytes accessed | tf_op | source)
XLA Modules:
  0.0 140.7 jit_solution(10491310042559270541)
XLA Ops:
  1.3 1.4 copy.9.ranks
  2.6 132.8 %shard_map.85 = (f32[2,2,512,128]{3,2,1,0:T(8,128)}, f32[2,2,192,128]{3,2,1,0:T(8,128)}, f32[2]{0:T(128)}) custom-call(bf16[2,2,2048,384]{3,2,1,0:T(8,128)(2,1)} %left_hbm.1, bf16[2,2,1536,512]{3,2,1,0:T(8,128)(2,1)} %right_hbm.1, s32[2,8,6]{2,1,0:T(8,128)} %copy.9.ranks, f32[2,2,192,128]{3,2,1,0:T(8,128)} %v_cur.1, f32[2,2,512,128]{3,2,1,0:T(8,128)} %u_prev_hbm.1, ...), custom_call_target="tpu_custom_call" | custom-call | flops 6442450944 | bytes 16777216 | tf_op jit(solution)/shard_map/pallas_call | solution.py:464
  135.4 2.3 %copy.14 = f32[2,2,512,128]{3,2,1,0:T(8,128)} copy(f32[2,2,512,128]{3,2,1,0:T(8,128)} %get-tuple-element.6) | data formatting | bytes 2097152
  137.7 1.8 %copy.15 = f32[2,2,192,128]{3,2,1,0:T(8,128)} copy(f32[2,2,192,128]{3,2,1,0:T(8,128)} %get-tuple-element.7) | data formatting | bytes 786432
  139.5 1.2 copy.16

commit v2 on v1

--- a/solution.py
+++ b/solution.py
@@ -146,31 +146,53 @@
     def left_copy(f, b):
         return remote(lbuf.at[f, b], lbuf.at[f, b], ls_sem.at[f, b], lr_sem.at[f, b], to(r, lax.rem(c + C - 1, C)))
 
+    def fill_right(f, b):
+        for p in range(2):
+            rbuf[f, b, p] = part[f, block_rows(b), p * nv : (p + 1) * nv].astype(BF16)
+        right_copy(f, b).start()
+
+    def fill_left(f, b):
+        for p in range(2):
+            lbuf[f, b, p] = part[f, block_rows(b), p * nv : (p + 1) * nv].astype(BF16)
+        left_copy(f, b).start()
+
     def images(f):
         def step(s, carry):
-            b = jnp.where(c < C // 2, C - 1 - s, s)
-            image_block(f, b)
-
-            @pl.when((c == 0) & (b > 0))
-            def _():
-                for p in range(2):
-                    rbuf[f, b, p] = part[f, block_rows(b), p * nv : (p + 1) * nv].astype(BF16)
-                right_copy(f, b).start()
-
-            @pl.when((c == C - 1) & (b < C - 1))
-            def _():
-                for p in range(2):
-                    lbuf[f, b, p] = part[f, block_rows(b), p * nv : (p + 1) * nv].astype(BF16)
-                left_copy(f, b).start()
+            image_block(f, jnp.where(c < C // 2, C - 1 - s, s))
+
+            if f == 0:
+
+                @pl.when((c == 0) & (s == 0))
+                def _():
+                    fill_right(0, C - 1)
+
+                @pl.when((c == C - 1) & (s == 0))
+                def _():
+                    fill_left(0, 0)
 
             return carry
 
         lax.fori_loop(0, C, step, 0)
 
-    def pass_sums(f, s):
+    def end_sums(f, s):
+        later = f * (C - 1) + s + 1
+        if later < F * (C - 1):
+            f_later, s_later = divmod(later, C - 1)
+
+            @pl.when(c == 0)
+            def _():
+                right_copy(f, C - 1 - s).wait_send()
+                fill_right(f_later, C - 1 - s_later)
+
+            @pl.when(c == C - 1)
+            def _():
+                left_copy(f, s).wait_send()
+                fill_left(f_later, s_later)
+
+    def sums_right(f, s, here):
         b = C - 1 - s
 
-        @pl.when((c > 0) & (c < b))
+        @pl.when(here & (c > 0) & (c < b))
         def _():
             right_copy(f, b).wait_recv()
             for p in range(2):
@@ -179,7 +201,8 @@
                 ).astype(BF16)
             right_copy(f, b).start()
 
-        @pl.when((c > s) & (c < C - 1))
+    def sums_left(f, s, here):
+        @pl.when(here & (c > s) & (c < C - 1))
         def _():
             left_copy(f, s).wait_recv()
             for p in range(2):
@@ -188,6 +211,20 @@
                 ).astype(BF16)
             left_copy(f, s).start()
 
+    def pass_sums(f, s, targets=False):
+        low = c < C // 2
+        high = c >= C // 2
+        end_sums(f, s)
+        sums_right(f, s, low)
+        sums_left(f, s, high)
+        if targets:
+            targets_left(f - 1, s + 1, low)
+            targets_right(f - 1, s + 1, high)
+            targets_right(f - 1, s + 1, low)
+            targets_left(f - 1, s + 1, high)
+        sums_left(f, s, low)
+        sums_right(f, s, high)
+
     def give_right(f, b):
         return remote(tbuf.at[f, b], tbuf.at[f, b], tr_sem.at[f, b], tt_sem.at[f, b], to(r, lax.rem(c + 1, C)))
 
@@ -228,8 +265,8 @@
 
         return total
 
-    def pass_targets(f, s, then):
-        @pl.when(c >= s)
+    def targets_right(f, s, here):
+        @pl.when(here & (c >= s))
         def _():
             b = c - s
             give_right(f, b).wait_recv()
@@ -238,9 +275,8 @@
             def _():
                 give_right(f, b).start()
 
-            then(b)
-
-        @pl.when(c + s < C)
+    def targets_left(f, s, here):
+        @pl.when(here & (c + s < C))
         def _():
             b = c + s
             give_left(f, b).wait_recv()
@@ -249,7 +285,18 @@
             def _():
                 give_left(f, b).start()
 
-            then(b)
+    def pass_targets(f, s):
+        targets_right(f, s, c >= 0)
+        targets_left(f, s, c >= 0)
+
+    def run_targets(s, run):
+        @pl.when(c >= s)
+        def _():
+            run(c - s)
+
+        @pl.when(c + s < C)
+        def _():
+            run(c + s)
 
     def norm_row(e, d):
         other = lax.rem(r + d, R)
@@ -362,6 +409,8 @@
             gather_start(f + 1, 0)
         loads[f][0].wait()
         project(f)
+        if f == 1:
+            pass_sums(0, 0)
         if f + 1 < F:
             gather_wait(f + 1, 0)
             gather_start(f + 1, 1)
@@ -373,36 +422,41 @@
                     gather_start(f + 1, m)
                 gather_wait(f + 1, m)
     load_u.wait()
-    nothing = lambda b: None
     total = jnp.zeros((8, nv), F32)
     for f in range(F):
         for s in range(C - 1):
-            pass_sums(f, s)
-            if f > 0:
-                pass_targets(f - 1, s + 1, nothing)
+            if f > 0 or s > 0 or F == 1:
+                pass_sums(f, s, f > 0)
         total = finish_sums(f, total)
     norm_start(0, total)
     count_u = F * 2 * ur * nv * R * C
     beta = norm_finish(0, count_u)
     inverse = 1.0 / beta
 
-    for f in range(F):
-        run = back_block(f, inverse)
-        if f < F - 1:
-            lax.fori_loop(0, C, lambda b, carry: (run(b), carry)[1], 0)
-        else:
+    last = F - 1
+    run = back_block(last, inverse)
+    steps = 0
+    for s in range(1, C):
+        pass_targets(last, s)
+        if s == 1:
+            for f in range(last):
+                early = back_block(f, inverse)
+                lax.fori_loop(0, C, lambda b, carry: (early(b), carry)[1], 0)
+                back_image(f)
+                halve_start(f, 0)
             run(c)
-            for s in range(1, C):
-                pass_targets(f, s, run)
-                if f > 0 and s < n:
-                    halve_next(f - 1, s - 1)
-            if f > 0:
-                for k in range(min(C - 1, n - 1), n):
-                    halve_next(f - 1, k)
-        back_image(f)
-        halve_start(f, 0)
+        elif steps < n:
+            for f in range(last):
+                halve_next(f, steps)
+            steps += 1
+        run_targets(s, run)
+    back_image(last)
+    halve_start(last, 0)
+    for k in range(steps, n):
+        for f in range(last):
+            halve_next(f, k)
     for k in range(n):
-        halve_next(F - 1, k)
+        halve_next(last, k)
     total = jnp.zeros((8, nv), F32)
     for f in range(F):
         for p in range(2):
@@ -423,11 +477,14 @@
     for f in range(F):
         for s in range(C):
 
-            @pl.when(c < s)
+            right_left = (c > 0) | (f == F - 1 and s == 1)
+            left_left = (c < C - 1) | (f == F - 1 and s == C - 2)
+
+            @pl.when((c < s) & right_left)
             def _():
                 right_copy(f, s).wait_send()
 
-            @pl.when(c > s)
+            @pl.when((c > s) & left_left)
             def _():
                 left_copy(f, s).wait_send()
 

time: 141 us -> 120 us (0.85)
  Pallas kernels: 133 us -> 112 us
    pallas_call x1, Pallas kernels: 133 us -> 112 us  [body(): pl.pallas_call(functools.partial(kernel, R, C), out_shape=(jax.ShapeDtype...]
where the time goes in v2:
time: 120 us
  Pallas kernels  112 us (93%)
  local copies, waits for them, and re-layouts  6.58 us (5%)
  between operations  1.29 us (1%)
    pallas_call x1, Pallas kernels, body(): pl.pallas_call(functools.partial(kernel, R, C), out_shape=(jax.ShapeDtype...  112 us
    unnamed x4, local copies, waits for them, and re-layouts  6.58 us

profile of v2, /device:TPU:0, one launch (start us, length us, event | category | flops | bytes accessed | tf_op | source)
XLA Modules:
  0.0 120.2 jit_solution(13859709842547980885)
XLA Ops:
  1.3 1.4 %copy.9.ranks = s32[2,8,6]{2,1,0:T(8,128)} copy(s32[2,8,6]{1,0,2:T(2,128)} %param.8) | data formatting | bytes 768 | tf_op args[2]
  2.6 112.4 %shard_map.85 = (f32[2,2,512,128]{3,2,1,0:T(8,128)}, f32[2,2,192,128]{3,2,1,0:T(8,128)}, f32[2]{0:T(128)}) custom-call(bf16[2,2,2048,384]{3,2,1,0:T(8,128)(2,1)} %left_hbm.1, bf16[2,2,1536,512]{3,2,1,0:T(8,128)(2,1)} %right_hbm.1, s32[2,8,6]{2,1,0:T(8,128)} %copy.9.ranks, f32[2,2,192,128]{3,2,1,0:T(8,128)} %v_cur.1, f32[2,2,512,128]{3,2,1,0:T(8,128)} %u_prev_hbm.1, ...), custom_call_target="tpu_custom_call" | custom-call | flops 6442450944 | bytes 16777216 | tf_op jit(solution)/shard_map/pallas_call | solution.py:521
  115.0 2.3 %copy.14 = f32[2,2,512,128]{3,2,1,0:T(8,128)} copy(f32[2,2,512,128]{3,2,1,0:T(8,128)} %get-tuple-element.6) | data formatting | bytes 2097152
  117.3 1.8 %copy.15 = f32[2,2,192,128]{3,2,1,0:T(8,128)} copy(f32[2,2,192,128]{3,2,1,0:T(8,128)} %get-tuple-element.7) | data formatting | bytes 786432
  119.0 1.2 copy.16

commit v3 on v2

--- a/solution.py
+++ b/solution.py
@@ -140,21 +140,21 @@
     def block_rows(b):
         return pl.ds(pl.multiple_of(b * ur, ur), ur)
 
-    def right_copy(f, b):
-        return remote(rbuf.at[f, b], rbuf.at[f, b], rs_sem.at[f, b], rr_sem.at[f, b], to(r, lax.rem(c + 1, C)))
-
-    def left_copy(f, b):
-        return remote(lbuf.at[f, b], lbuf.at[f, b], ls_sem.at[f, b], lr_sem.at[f, b], to(r, lax.rem(c + C - 1, C)))
-
-    def fill_right(f, b):
-        for p in range(2):
-            rbuf[f, b, p] = part[f, block_rows(b), p * nv : (p + 1) * nv].astype(BF16)
-        right_copy(f, b).start()
-
-    def fill_left(f, b):
-        for p in range(2):
-            lbuf[f, b, p] = part[f, block_rows(b), p * nv : (p + 1) * nv].astype(BF16)
-        left_copy(f, b).start()
+    def right_copy(f, b, p):
+        here = rbuf.at[f, b, p]
+        return remote(here, here, rs_sem.at[f, b, p], rr_sem.at[f, b, p], to(r, lax.rem(c + 1, C)))
+
+    def left_copy(f, b, p):
+        here = lbuf.at[f, b, p]
+        return remote(here, here, ls_sem.at[f, b, p], lr_sem.at[f, b, p], to(r, lax.rem(c + C - 1, C)))
+
+    def fill_right(f, b, p):
+        rbuf[f, b, p] = part[f, block_rows(b), p * nv : (p + 1) * nv].astype(BF16)
+        right_copy(f, b, p).start()
+
+    def fill_left(f, b, p):
+        lbuf[f, b, p] = part[f, block_rows(b), p * nv : (p + 1) * nv].astype(BF16)
+        left_copy(f, b, p).start()
 
     def images(f):
         def step(s, carry):
@@ -164,11 +164,13 @@
 
                 @pl.when((c == 0) & (s == 0))
                 def _():
-                    fill_right(0, C - 1)
+                    for p in range(2):
+                        fill_right(0, C - 1, p)
 
                 @pl.when((c == C - 1) & (s == 0))
                 def _():
-                    fill_left(0, 0)
+                    for p in range(2):
+                        fill_left(0, 0, p)
 
             return carry
 
@@ -181,35 +183,37 @@
 
             @pl.when(c == 0)
             def _():
-                right_copy(f, C - 1 - s).wait_send()
-                fill_right(f_later, C - 1 - s_later)
+                for p in range(2):
+                    right_copy(f, C - 1 - s, p).wait_send()
+                    fill_right(f_later, C - 1 - s_later, p)
 
             @pl.when(c == C - 1)
             def _():
-                left_copy(f, s).wait_send()
-                fill_left(f_later, s_later)
+                for p in range(2):
+                    left_copy(f, s, p).wait_send()
+                    fill_left(f_later, s_later, p)
 
     def sums_right(f, s, here):
         b = C - 1 - s
 
         @pl.when(here & (c > 0) & (c < b))
         def _():
-            right_copy(f, b).wait_recv()
             for p in range(2):
+                right_copy(f, b, p).wait_recv()
                 rbuf[f, b, p] = (
                     rbuf[f, b, p].astype(F32) + part[f, block_rows(b), p * nv : (p + 1) * nv]
                 ).astype(BF16)
-            right_copy(f, b).start()
+                right_copy(f, b, p).start()
 
     def sums_left(f, s, here):
         @pl.when(here & (c > s) & (c < C - 1))
         def _():
-            left_copy(f, s).wait_recv()
             for p in range(2):
+                left_copy(f, s, p).wait_recv()
                 lbuf[f, s, p] = (
                     lbuf[f, s, p].astype(F32) + part[f, block_rows(s), p * nv : (p + 1) * nv]
                 ).astype(BF16)
-            left_copy(f, s).start()
+                left_copy(f, s, p).start()
 
     def pass_sums(f, s, targets=False):
         low = c < C // 2
@@ -225,65 +229,65 @@
         sums_left(f, s, low)
         sums_right(f, s, high)
 
-    def give_right(f, b):
-        return remote(tbuf.at[f, b], tbuf.at[f, b], tr_sem.at[f, b], tt_sem.at[f, b], to(r, lax.rem(c + 1, C)))
-
-    def give_left(f, b):
-        return remote(tbuf.at[f, b], tbuf.at[f, b], tl_sem.at[f, b], tt_sem.at[f, b], to(r, lax.rem(c + C - 1, C)))
+    def give_right(f, b, p):
+        here = tbuf.at[f, b, p]
+        return remote(here, here, tr_sem.at[f, b, p], tt_sem.at[f, b, p], to(r, lax.rem(c + 1, C)))
+
+    def give_left(f, b, p):
+        here = tbuf.at[f, b, p]
+        return remote(here, here, tl_sem.at[f, b, p], tt_sem.at[f, b, p], to(r, lax.rem(c + C - 1, C)))
 
     def squares(value):
         return jnp.sum((value * value).reshape(-1, 8, nv), axis=0)
 
     def finish_sums(f, total):
-        @pl.when(c > 0)
-        def _():
-            right_copy(f, c).wait_recv()
-            for p in range(2):
-                lanes = slice(p * nv, (p + 1) * nv)
+        for p in range(2):
+            lanes = slice(p * nv, (p + 1) * nv)
+
+            @pl.when(c > 0)
+            def _():
+                right_copy(f, c, p).wait_recv()
                 part[f, block_rows(c), lanes] = part[f, block_rows(c), lanes] + rbuf[f, c, p].astype(F32)
 
-        @pl.when(c < C - 1)
-        def _():
-            left_copy(f, c).wait_recv()
-            for p in range(2):
-                lanes = slice(p * nv, (p + 1) * nv)
+            @pl.when(c < C - 1)
+            def _():
+                left_copy(f, c, p).wait_recv()
                 part[f, block_rows(c), lanes] = part[f, block_rows(c), lanes] + lbuf[f, c, p].astype(F32)
 
-        for p in range(2):
-            value = part[f, block_rows(c), p * nv : (p + 1) * nv] - alpha_prev[0] * u_prev[f, p]
+            value = part[f, block_rows(c), lanes] - alpha_prev[0] * u_prev[f, p]
             u_next[f, p] = value
             tbuf[f, c, p] = value.astype(BF16)
+
+            @pl.when(c < C - 1)
+            def _():
+                give_right(f, c, p).start()
+
+            @pl.when(c > 0)
+            def _():
+                give_left(f, c, p).start()
+
             total = total + squares(value)
-
-        @pl.when(c < C - 1)
-        def _():
-            give_right(f, c).start()
-
-        @pl.when(c > 0)
-        def _():
-            give_left(f, c).start()
-
         return total
 
     def targets_right(f, s, here):
         @pl.when(here & (c >= s))
         def _():
-            b = c - s
-            give_right(f, b).wait_recv()
-
-            @pl.when(c < C - 1)
-            def _():
-                give_right(f, b).start()
+            for p in range(2):
+                give_right(f, c - s, p).wait_recv()
+
+                @pl.when(c < C - 1)
+                def _():
+                    give_right(f, c - s, p).start()
 
     def targets_left(f, s, here):
         @pl.when(here & (c + s < C))
         def _():
-            b = c + s
-            give_left(f, b).wait_recv()
-
-            @pl.when(c > 0)
-            def _():
-                give_left(f, b).start()
+            for p in range(2):
+                give_left(f, c + s, p).wait_recv()
+
+                @pl.when(c > 0)
+                def _():
+                    give_left(f, c + s, p).start()
 
     def pass_targets(f, s):
         targets_right(f, s, c >= 0)
@@ -437,19 +441,28 @@
     run = back_block(last, inverse)
     steps = 0
     for s in range(1, C):
-        pass_targets(last, s)
+        if s != 2:
+            pass_targets(last, s)
         if s == 1:
             for f in range(last):
                 early = back_block(f, inverse)
                 lax.fori_loop(0, C, lambda b, carry: (early(b), carry)[1], 0)
+                if C > 2 and f == 0:
+                    pass_targets(last, 2)
                 back_image(f)
                 halve_start(f, 0)
             run(c)
-        elif steps < n:
-            for f in range(last):
-                halve_next(f, steps)
-            steps += 1
-        run_targets(s, run)
+            run_targets(1, run)
+            if C > 2:
+                for f in range(last):
+                    halve_next(f, 0)
+                run_targets(2, run)
+                steps = min(2, n)
+                for f in range(last):
+                    for k in range(1, steps):
+                        halve_next(f, k)
+        if s > 2:
+            run_targets(s, run)
     back_image(last)
     halve_start(last, 0)
     for k in range(steps, n):
@@ -482,19 +495,23 @@
 
             @pl.when((c < s) & right_left)
             def _():
-                right_copy(f, s).wait_send()
+                for p in range(2):
+                    right_copy(f, s, p).wait_send()
 
             @pl.when((c > s) & left_left)
             def _():
-                left_copy(f, s).wait_send()
+                for p in range(2):
+                    left_copy(f, s, p).wait_send()
 
             @pl.when((s <= c) & (c < C - 1))
             def _():
-                give_right(f, s).wait_send()
+                for p in range(2):
+                    give_right(f, s, p).wait_send()
 
             @pl.when((s >= c) & (c > 0))
             def _():
-                give_left(f, s).wait_send()
+                for p in range(2):
+                    give_left(f, s, p).wait_send()
 
         for p in range(2):
             for k in range(n):
@@ -547,13 +564,13 @@
             dma((2 * F + 1,)),
             dma((F, 2, n)),
             dma((F, 2, n)),
-            dma((F, C)),
-            dma((F, C)),
-            dma((F, C)),
-            dma((F, C)),
-            dma((F, C)),
-            dma((F, C)),
-            dma((F, C)),
+            dma((F, C, 2)),
+            dma((F, C, 2)),
+            dma((F, C, 2)),
+            dma((F, C, 2)),
+            dma((F, C, 2)),
+            dma((F, C, 2)),
+            dma((F, C, 2)),
             dma((F, 2, n)),
             dma((F, 2, n)),
             dma((2, R)),

time: 120 us -> 123 us (1.025)
  Pallas kernels: 112 us -> 115 us
    pallas_call x1, Pallas kernels: 112 us -> 115 us  [body(): pl.pallas_call(functools.partial(kernel, R, C), out_shape=(jax.ShapeDtype...]
where the time goes in v3:
time: 123 us; the launch traced here: 122 us
  Pallas kernels  115 us (93%)
  local copies, waits for them, and re-layouts  6.58 us (5%)
  between operations  1.29 us (1%)
    pallas_call x1, Pallas kernels, body(): pl.pallas_call(functools.partial(kernel, R, C), out_shape=(jax.ShapeDtype...  115 us
    unnamed x4, local copies, waits for them, and re-layouts  6.58 us

profile of v3, /device:TPU:0, one launch (start us, length us, event | category | flops | bytes accessed | tf_op | source)
XLA Modules:
  0.0 122.4 jit_solution(5209887452273137463)
XLA Ops:
  1.3 1.4 %copy.9.ranks = s32[2,8,6]{2,1,0:T(8,128)} copy(s32[2,8,6]{1,0,2:T(2,128)} %param.8) | data formatting | bytes 768 | tf_op args[2]
  2.6 114.5 %shard_map.85 = (f32[2,2,512,128]{3,2,1,0:T(8,128)}, f32[2,2,192,128]{3,2,1,0:T(8,128)}, f32[2]{0:T(128)}) custom-call(bf16[2,2,2048,384]{3,2,1,0:T(8,128)(2,1)} %left_hbm.1, bf16[2,2,1536,512]{3,2,1,0:T(8,128)(2,1)} %right_hbm.1, s32[2,8,6]{2,1,0:T(8,128)} %copy.9.ranks, f32[2,2,192,128]{3,2,1,0:T(8,128)} %v_cur.1, f32[2,2,512,128]{3,2,1,0:T(8,128)} %u_prev_hbm.1, ...), custom_call_target="tpu_custom_call" | custom-call | flops 6442450944 | bytes 16777216 | tf_op jit(solution)/shard_map/pallas_call | solution.py:538
  117.2 2.3 %copy.14 = f32[2,2,512,128]{3,2,1,0:T(8,128)} copy(f32[2,2,512,128]{3,2,1,0:T(8,128)} %get-tuple-element.6) | data formatting | bytes 2097152
  119.5 1.8 %copy.15 = f32[2,2,192,128]{3,2,1,0:T(8,128)} copy(f32[2,2,192,128]{3,2,1,0:T(8,128)} %get-tuple-element.7) | data formatting | bytes 786432
  121.2 1.2 copy.16

commit v4 on v2

--- a/solution.py
+++ b/solution.py
@@ -408,9 +408,11 @@
         if f + 1 < F:
             gather_start(f + 1, 0)
         loads[f][0].wait()
-        project(f)
         if f == 1:
             pass_sums(0, 0)
+        project(f)
+        if f == 1 and C > 2:
+            pass_sums(0, 1)
         if f + 1 < F:
             gather_wait(f + 1, 0)
             gather_start(f + 1, 1)
@@ -425,7 +427,7 @@
     total = jnp.zeros((8, nv), F32)
     for f in range(F):
         for s in range(C - 1):
-            if f > 0 or s > 0 or F == 1:
+            if f > 0 or s > 1 or F == 1:
                 pass_sums(f, s, f > 0)
         total = finish_sums(f, total)
     norm_start(0, total)
@@ -437,19 +439,28 @@
     run = back_block(last, inverse)
     steps = 0
     for s in range(1, C):
-        pass_targets(last, s)
+        if s != 2:
+            pass_targets(last, s)
         if s == 1:
             for f in range(last):
                 early = back_block(f, inverse)
                 lax.fori_loop(0, C, lambda b, carry: (early(b), carry)[1], 0)
+                if C > 2 and f == 0:
+                    pass_targets(last, 2)
                 back_image(f)
                 halve_start(f, 0)
             run(c)
-        elif steps < n:
-            for f in range(last):
-                halve_next(f, steps)
-            steps += 1
-        run_targets(s, run)
+            run_targets(1, run)
+            if C > 2:
+                for f in range(last):
+                    halve_next(f, 0)
+                run_targets(2, run)
+                steps = min(2, n)
+                for f in range(last):
+                    for k in range(1, steps):
+                        halve_next(f, k)
+        if s > 2:
+            run_targets(s, run)
     back_image(last)
     halve_start(last, 0)
     for k in range(steps, n):

time: 120 us -> 124 us (1.033)
  Pallas kernels: 112 us -> 115 us
    pallas_call x1, Pallas kernels: 112 us -> 115 us  [body(): pl.pallas_call(functools.partial(kernel, R, C), out_shape=(jax.ShapeDtype...]
where the time goes in v4:
time: 124 us; the launch traced here: 123 us
  Pallas kernels  115 us (93%)
  local copies, waits for them, and re-layouts  6.58 us (5%)
  between operations  1.29 us (1%)
    pallas_call x1, Pallas kernels, body(): pl.pallas_call(functools.partial(kernel, R, C), out_shape=(jax.ShapeDtype...  115 us
    unnamed x4, local copies, waits for them, and re-layouts  6.58 us

profile of v4, /device:TPU:0, one launch (start us, length us, event | category | flops | bytes accessed | tf_op | source)
XLA Modules:
  0.0 123.3 jit_solution(16958359358874870924)
XLA Ops:
  1.3 1.4 %copy.9.ranks = s32[2,8,6]{2,1,0:T(8,128)} copy(s32[2,8,6]{1,0,2:T(2,128)} %param.8) | data formatting | bytes 768 | tf_op args[2]
  2.6 115.4 %shard_map.85 = (f32[2,2,512,128]{3,2,1,0:T(8,128)}, f32[2,2,192,128]{3,2,1,0:T(8,128)}, f32[2]{0:T(128)}) custom-call(bf16[2,2,2048,384]{3,2,1,0:T(8,128)(2,1)} %left_hbm.1, bf16[2,2,1536,512]{3,2,1,0:T(8,128)(2,1)} %right_hbm.1, s32[2,8,6]{2,1,0:T(8,128)} %copy.9.ranks, f32[2,2,192,128]{3,2,1,0:T(8,128)} %v_cur.1, f32[2,2,512,128]{3,2,1,0:T(8,128)} %u_prev_hbm.1, ...), custom_call_target="tpu_custom_call" | custom-call | flops 6442450944 | bytes 16777216 | tf_op jit(solution)/shard_map/pallas_call | solution.py:532
  118.1 2.3 %copy.14 = f32[2,2,512,128]{3,2,1,0:T(8,128)} copy(f32[2,2,512,128]{3,2,1,0:T(8,128)} %get-tuple-element.6) | data formatting | bytes 2097152
  120.3 1.8 %copy.15 = f32[2,2,192,128]{3,2,1,0:T(8,128)} copy(f32[2,2,192,128]{3,2,1,0:T(8,128)} %get-tuple-element.7) | data formatting | bytes 786432
  122.1 1.2 copy.16
